TPU v7x, 768 devices: a whole 4x8x12 slice. The times are simulated.
768 devices in a mesh: dp: 192 (over x, y_lo, z, core), mp: 4 (over y_hi).
Axes of the slice: x: 4, y: 8 (y_hi: 4, y_lo: 2; y = y_hi * 2 + y_lo), z: 12, core: 2. Of those that a mesh axis runs over, the one named last changes fastest.
Arguments:
- activations: bfloat16 [512, 9216], P('mp', 'dp'), may hold values from -6 to 6
- block_values: bfloat16 [384, 20, 128, 128], P('dp'), may hold values from -0.125 to 0.125
- block_rows: int32 [384, 20], P('dp'), may hold values from 0 to 71, all different within a row
- cotangent: bfloat16 [512, 49152], P('mp', 'dp'), may hold values from -6 to 6
Outputs:
- gelu_out: bfloat16 [512, 49152], P('mp', 'dp')
- input_grad: bfloat16 [512, 9216], P('mp', 'dp')
- block_grad: float32 [384, 20, 128, 128], P('dp', 'mp')
Inputs may be any that keep to these rules, and one draw needn't show every extreme that they name: `block_rows`: the 20 entries of each column block are different block rows; every block row is named somewhere.
All inputs are finite; a program needn't handle non-finite values.
Results may differ from a plain program's by a relative error of at most 0.0049.
Values may be sent and summed in bfloat16 or wider, within the bound.
A program may use at most 64 MiB of HBM per device.

v0:
```python
import jax
import jax.numpy as jnp
from jax import lax
from jax.sharding import PartitionSpec as P


def gelu_tanh(values):
    return jax.nn.gelu(values, approximate=True)


def body(activations, block_values, block_rows, cotangent):
    rows_here = activations.shape[0]
    col_blocks = block_values.shape[0]
    slot_count = block_values.shape[1]
    block_size = block_values.shape[2]
    total_slots = col_blocks * slot_count
    x_full = lax.all_gather(activations, "dp", axis=1, tiled=True)
    row_blocks = x_full.shape[1] // block_size
    rows_flat = block_rows.reshape(-1)
    picked_rows = jnp.take(x_full.reshape(rows_here, row_blocks, block_size), rows_flat, axis=1)
    picked_rows = picked_rows.reshape(rows_here, col_blocks, slot_count, block_size)
    pre_act = jnp.einsum(
        "tcki,ckij->tcj", picked_rows, block_values, preferred_element_type=jnp.float32
    )
    gelu_out = gelu_tanh(pre_act).astype(jnp.bfloat16).reshape(rows_here, col_blocks * block_size)
    unused, pull_back = jax.vjp(gelu_tanh, pre_act)
    cot_blocks = cotangent.reshape(rows_here, col_blocks, block_size).astype(jnp.float32)
    slopes = pull_back(cot_blocks)[0].astype(jnp.bfloat16)
    contrib = jnp.einsum("tcj,ckij->tcki", slopes, block_values, preferred_element_type=jnp.float32)
    contrib = contrib.reshape(rows_here, total_slots, block_size)
    one_hot = (rows_flat[:, None] == jnp.arange(row_blocks, dtype=jnp.int32)[None, :]).astype(
        jnp.float32
    )
    dx_term = jnp.einsum("tmi,mr->tri", contrib, one_hot, precision=lax.Precision.HIGHEST)
    dx_term = dx_term.reshape(rows_here, row_blocks * block_size)
    input_grad = lax.psum_scatter(dx_term, "dp", scatter_dimension=1, tiled=True).astype(
        jnp.bfloat16
    )
    partial_grad = jnp.einsum(
        "tcki,tcj->ckij", picked_rows, slopes, preferred_element_type=jnp.float32
    )
    block_grad = lax.psum_scatter(partial_grad, "mp", scatter_dimension=1, tiled=True)
    return (gelu_out, input_grad, block_grad)


def solution(mesh):
    in_specs = (P("mp", "dp"), P("dp", None, None, None), P("dp", None), P("mp", "dp"))
    out_specs = (P("mp", "dp"), P("mp", "dp"), P("dp", "mp", None, None))
    return jax.shard_map(body, mesh=mesh, in_specs=in_specs, out_specs=out_specs, check_vma=False)
```

profile of v0, /device:TPU:1, one launch (start us, length us, event | category | flops | bytes accessed | tf_op | source)
XLA Modules:
  0.0 1326.0 jit_solution(6742355362006776580)
XLA Ops:
  7.2 0.0 copy-start
  7.2 0.0 all-gather.2.cloned.1.call-start
  7.2 0.7 all-gather.2.cloned.1.call-update
  7.9 0.0 all-reduce.3.cloned.1.call-start
  8.0 0.8 reshape.65
  8.7 0.9 copy.17
  9.7 0.7 compare_and_fusion
  10.4 327.3 %all-gather.2.cloned.1.call-done = bf16[128,9216]{0,1:T(8,128)(2,1)} async-done(((bf16[128,48]{0,1:T(8,128)(2,1)}), bf16[128,9216]{0,1:T(8,128)(2,1)}) %all-gather.2.cloned.1.call-update) | async-done | bytes 2359312 | tf_op jit(solution)/shard_map/all_gather | solution.py:17
  337.7 2.5 gather_fusion
  340.2 0.0 copy-done
  340.2 0.7 fusion.16
  340.9 2.1 fusion.5
  343.0 0.0 copy-start.1
  343.0 0.0 all-reduce.3.cloned.1.call-update
  343.0 0.0 reduce-scatter.5.cloned.1.call-start
  343.1 0.6 copy-done.1
  343.7 0.1 reshape.67
  343.7 0.6 fusion.18
  344.3 5.9 fusion.2
  350.2 6.1 copy.30
  356.3 0.0 reduce-scatter.5.cloned.1.call-update
  356.3 1.3 dynamic-slice
  358.3 0.7 copy.22
  359.0 106.1 %all-reduce.3.cloned.1.call-done = f32[2,20,128,128]{3,2,1,0:T(8,128)} async-done(((f32[2,20,128,128]{3,2,1,0:T(8,128)}), f32[2,20,128,128]{3,2,1,0:T(8,128)}) %all-reduce.3.cloned.1.call-update) | async-done | bytes 2621456
  465.1 2.0 constant_dynamic-slice_fusion
  467.0 851.1 %reduce-scatter.5.cloned.1.call-done = f32[128,48]{0,1:T(8,128)} async-done(((f32[128,9216]{0,1:T(8,128)}), f32[128,48]{0,1:T(8,128)}) %reduce-scatter.5.cloned.1.call-update) | async-done | bytes 24592 | tf_op jit(solution)/shard_map/reduce_scatter | solution.py:36
  1318.1 1.3 convert_element_type.20
  (2 shorter events, 0.0 us)
Async XLA Ops:
  7.2 333.0 %copy-start = (bf16[2,20,128,128]{3,2,1,0:T(8,128)(2,1)S(1)}, bf16[2,20,128,128]{3,2,1,0:T(8,128)(2,1)}, u32[]{:S(2)}) copy-start(bf16[2,20,128,128]{3,2,1,0:T(8,128)(2,1)} %param.5) | copy-start | bytes 3932164
  7.2 330.5 %all-gather.2.cloned.1.call-start = ((), (), s32[]{:S(2)}) async-start(), calls=%async_computation.1 | async-start | bytes 2371584 | tf_op jit(solution)/shard_map/all_gather | solution.py:17
  7.9 457.2 %all-reduce.3.cloned.1.call-start = ((), (), s32[]{:S(2)}) async-start(), calls=%async_computation.3 | async-start | bytes 5242880
  343.0 0.7 copy-start.1
  343.0 975.1 %reduce-scatter.5.cloned.1.call-start = ((), (), s32[]{:S(2)}) async-start(), calls=%async_computation.2 | async-start | bytes 4743168 | tf_op jit(solution)/shard_map/reduce_scatter | solution.py:36
Sparse Core Ops, SparseCore 0:
  10.5 327.1 all-gather.1
  343.1 121.8 all-reduce.2
  468.2 849.9 reduce-scatter.4
where the time goes:
time: 1330 us
  waiting for transfers between devices  1290 us (97%)
  local copies, waits for them, and re-layouts  14.9 us (1%)
  between operations  14.5 us (1%)
    reduce_scatter x1, waiting for transfers between devices, body(): lax.psum_scatter(dx_term, 'dp', scatter_dimension=1, tiled=True)  851 us
    all_gather x1, waiting for transfers between devices, body(): x_full = lax.all_gather(activations, 'dp', axis=1, tiled=True)  327 us
    unnamed x4, waiting for transfers between devices  107 us
  transfers between devices with their start and end apart: 3, of which 3 were waited for; matrix products, arithmetic and copies ran while one was open for 1% of the time, Pallas kernels for 0%

commit v1 on v0

v1 whole, which is shorter than its diff:
```python
import functools

import jax
import jax.numpy as jnp
from jax import lax
from jax.experimental import pallas as pl
from jax.experimental.pallas import tpu as pltpu
from jax.sharding import PartitionSpec as P

NX, NY, NZ, NC, NM = 4, 2, 12, 2, 4
BLK, KB, RB, CB = 128, 20, 72, 2
SH = 48
ZB = 4
NB = NZ // ZB
OWN = KB // NM
FAR_FIRST = (2, 1, 3)
Z_ORDER = (1, 11, 2, 10, 3, 9, 4, 8, 5, 7, 6)
F32, BF16 = jnp.float32, jnp.bfloat16
C0 = 0.7978845608028654
C1 = 0.044715


def coords():
    d = lax.axis_index("dp")
    c = lax.rem(d, NC)
    z = lax.rem(lax.div(d, NC), NZ)
    y = lax.rem(lax.div(d, NC * NZ), NY)
    x = lax.div(d, NC * NZ * NY)
    return x, y, z, c, lax.axis_index("mp")


def device(x, y, z, c, m):
    return (((x * NY + y) * NZ + z) * NC + c, m)


def remote(src, dst, send, recv, to):
    return pltpu.make_async_remote_copy(
        src_ref=src, dst_ref=dst, send_sem=send, recv_sem=recv,
        device_id=to, device_id_type=pl.DeviceIdType.MESH,
    )


def kernel(
    rows_ref, inv_ref, xt_ref, cot_ref, w_hbm,
    gelu_ref, dx_ref, bg_ref,
    X, W, XF, XP, SL, D, S, XS, XR, OX, YS, YR, OY, ZS, ZR,
    GS1, GR1, GS2, GR2, GP,
    wsem, zs, zr, ys, yr, xs, xr, bs, br,
    ss, sr, rxs, rxr, rys, ryr, rzs, rzr, g1s, g1r, g2s, g2r,
):
    x, y, z, c, m = coords()
    oy, oc = 1 - y, 1 - c
    xa = [x] + [lax.rem(x + j, NX) for j in range(1, NX)]
    za = [z] + [lax.rem(z + k, NZ) for k in range(1, NZ)]
    m1, m2, m3 = (lax.rem(m + k, NM) for k in (1, 2, 3))
    to_x = [None] + [device(xa[j], y, z, c, m) for j in range(1, NX)]
    to_z = [None] + [device(x, y, za[k], c, m) for k in range(1, NZ)]
    to_y = device(x, oy, z, c, m)
    to_c = device(x, y, z, oc, m)
    to_up, to_down = device(x, y, z, c, m1), device(x, y, z, c, m3)

    wcopy = pltpu.make_async_copy(w_hbm, W.at[:, pl.ds(0, KB)], wsem)
    wcopy.start()

    barrier = pltpu.get_barrier_semaphore()
    partners = to_z[1:] + to_x[1:] + [to_y, to_c, to_up, to_down]
    for d in partners:
        pl.semaphore_signal(barrier, inc=1, device_id=d, device_id_type=pl.DeviceIdType.MESH)
    pl.semaphore_wait(barrier, len(partners))

    started = []

    def go(copy):
        copy.start()
        started.append(copy)

    for k in Z_ORDER:
        go(remote(xt_ref, X.at[x, y, z, c], zs.at[k - 1], zr.at[z], to_z[k]))
    X[x, y, z, c] = xt_ref[...]
    b0 = lax.div(z, ZB)
    blocks = [lax.rem(b0 + i, NB) for i in range(NB)]

    def part(xx, yy, i, cc):
        return X.at[xx, yy, pl.ds(blocks[i] * ZB, ZB), cc]

    def spread(yy, p, i):
        piece = part(x, yy, i, c)
        for j in FAR_FIRST:
            go(remote(piece, piece, xs.at[j - 1, p, i], xr.at[j - 1, p, i], to_x[j]))
        go(remote(piece, piece, bs.at[0, p, i], br.at[0, p, i], to_c))

    def from_y(i):
        piece = part(x, oy, i, c)
        remote(piece, piece, ys.at[i], yr.at[i], to_y).wait_recv()
        spread(oy, 1, i)

    for i in range(NB):
        for n in range(ZB):
            zz = blocks[i] * ZB + n

            @pl.when(zz != z)
            def _():
                piece = X.at[x, y, zz, c]
                remote(piece, piece, zs.at[0], zr.at[zz], to_y).wait_recv()

        piece = part(x, y, i, c)
        go(remote(piece, piece, ys.at[i], yr.at[i], to_y))
        spread(y, 0, i)
        if i:
            from_y(i - 1)
    from_y(NB - 1)
    wcopy.wait()
    for cb in range(CB):
        W[cb, KB] = jnp.zeros((BLK, BLK), BF16)
    for p in range(NY):
        for i in range(NB):
            for j in (1, 3, 2):
                piece = part(xa[NX - j], (y, oy)[p], i, c)
                remote(piece, piece, xs.at[j - 1, p, i], xr.at[j - 1, p, i], to_y).wait_recv()
                go(remote(piece, piece, bs.at[j, p, i], br.at[j, p, i], to_c))
    for p in range(NY):
        for i in range(NB):
            for j in (0, 1, 3, 2):
                piece = part(xa[(NX - j) % NX], (y, oy)[p], i, oc)
                remote(piece, piece, bs.at[j, p, i], br.at[j, p, i], to_c).wait_recv()

    XF[...] = X[...].reshape(RB, BLK, BLK)
    for cb in range(CB):
        for k in range(KB):
            XP[cb, pl.ds(k * BLK, BLK)] = XF[rows_ref[cb, k]]
    for cb in range(CB):
        cols = pl.ds(cb * BLK, BLK)
        v = lax.dot_general(
            XP[cb], W[cb, :KB].reshape(KB * BLK, BLK), (((0,), (0,)), ((), ())),
            preferred_element_type=F32,
        )
        t = jnp.tanh(C0 * (v + C1 * (v * v * v)))
        gelu_ref[:, cols] = (0.5 * v * (1.0 + t)).astype(BF16)
        slope = 0.5 * (1.0 + t) + 0.5 * v * (1.0 - t * t) * (C0 * (1.0 + 3.0 * C1 * (v * v)))
        SL[:, cols] = (cot_ref[:, cols].astype(F32) * slope).astype(BF16)

    def grads(cb, group):
        return jnp.dot(
            XP[cb, pl.ds(group * (OWN * BLK), OWN * BLK)], SL[:, cb * BLK : (cb + 1) * BLK],
            preferred_element_type=F32,
        )

    GS1[0] = grads(0, m2).astype(BF16)
    go(remote(GS1.at[0], GR1.at[0], g1s.at[0], g1r.at[0], to_up))
    GS1[1] = grads(1, m2).astype(BF16)
    go(remote(GS1.at[1], GR1.at[1], g1s.at[1], g1r.at[1], to_down))
    GS2[0, 1] = grads(1, m1).astype(BF16)
    go(remote(GS2.at[0, 1], GR2.at[0, 1], g2s.at[0, 1], g2r.at[0, 1], to_up))
    GS2[1, 0] = grads(0, m3).astype(BF16)
    go(remote(GS2.at[1, 0], GR2.at[1, 0], g2s.at[1, 0], g2r.at[1, 0], to_down))
    GP[0] = grads(0, m1)
    GP[1] = grads(1, m3)

    def terms(j):
        xx = xa[j]

        def step(g, carry):
            made = []
            for n in range(3):
                r = xx * (RB // NX) + g * 3 + n
                pair = jnp.concatenate([W[0, inv_ref[0, r]], W[1, inv_ref[1, r]]], axis=1)
                made.append(
                    lax.dot_general(pair, SL[...], (((1,), (1,)), ((), ())), preferred_element_type=F32)
                )
            both = jnp.concatenate(made, axis=0).reshape(ZB, NC, SH, BLK).astype(BF16)
            D[xx, lax.div(g, NB), pl.ds(lax.rem(g, NB) * ZB, ZB)] = both
            return carry

        lax.fori_loop(0, NY * NB, step, 0)
        go(remote(D.at[xx, :, :, oc], S.at[j], ss.at[j], sr.at[j], to_c))

    def paired(j):
        remote(D.at[xa[j], :, :, oc], S.at[j], ss.at[j], sr.at[j], to_c).wait_recv()

    def both_cores(j, p):
        yy = (y, oy)[p]
        return D[xa[j], yy, :, c].astype(F32) + S[j, yy].astype(F32)

    def along_x(j):
        paired(j)
        for p in (1, 0):
            XS[j - 1, p] = both_cores(j, p).astype(BF16)
            go(remote(XS.at[j - 1, p], XR.at[j - 1, p], rxs.at[j - 1, p], rxr.at[j - 1, p], to_x[j]))

    terms(2)
    terms(1)
    along_x(2)
    terms(3)
    along_x(1)
    terms(0)
    along_x(3)
    paired(0)
    for p in range(NY):
        OX[p] = both_cores(0, p)
    for cb in range(CB):
        bg_ref[cb] = grads(cb, m).reshape(OWN, BLK, BLK)

    def from_x(p):
        total = OX[p]
        for j in range(1, NX):
            remote(XS.at[j - 1, p], XR.at[j - 1, p], rxs.at[j - 1, p], rxr.at[j - 1, p], to_y).wait_recv()
            total = total + XR[j - 1, p].astype(F32)
        return total

    def second(side, cb, to):
        remote(GS1.at[cb], GR1.at[cb], g1s.at[cb], g1r.at[cb], to).wait_recv()
        GS2[side, cb] = (GP[cb] + GR1[cb].astype(F32)).astype(BF16)
        go(remote(GS2.at[side, cb], GR2.at[side, cb], g2s.at[side, cb], g2r.at[side, cb], to))

    second(0, 0, to_up)
    second(1, 1, to_down)
    YS[...] = from_x(1).astype(BF16)
    go(remote(YS, YR, rys, ryr, to_y))
    OY[...] = from_x(0)
    remote(YS, YR, rys, ryr, to_y).wait_recv()
    OY[...] = OY[...] + YR[...].astype(F32)
    ZS[...] = OY[...].astype(BF16)
    for k in Z_ORDER:
        go(remote(ZS.at[za[k]], ZR.at[k - 1], rzs.at[k - 1], rzr.at[k - 1], to_z[k]))
    dx = OY[z]
    for k in Z_ORDER:
        remote(ZS.at[za[k]], ZR.at[k - 1], rzs.at[k - 1], rzr.at[k - 1], to_y).wait_recv()
        dx = dx + ZR[k - 1].astype(F32)
    dx_ref[...] = dx.astype(BF16)

    for cb in range(CB):
        total = bg_ref[cb]
        for side in range(2):
            remote(GS2.at[side, cb], GR2.at[side, cb], g2s.at[side, cb], g2r.at[side, cb], to_up).wait_recv()
            total = total + GR2[side, cb].astype(F32).reshape(OWN, BLK, BLK)
        bg_ref[cb] = total
    for copy in started:
        copy.wait_send()


def body(activations, block_values, block_rows, cotangent):
    tokens = activations.shape[0]
    slots = jnp.arange(KB, dtype=jnp.int32) - KB
    named = block_rows[:, None, :] == jnp.arange(RB, dtype=jnp.int32)[None, :, None]
    inverse = KB + jnp.sum(jnp.where(named, slots, 0), axis=2, dtype=jnp.int32)
    smem, vmem = pl.BlockSpec(memory_space=pltpu.SMEM), pl.BlockSpec(memory_space=pltpu.VMEM)
    dma = pltpu.SemaphoreType.DMA
    column = (OWN * BLK, BLK)
    gelu_out, dx, block_grad = pl.pallas_call(
        kernel,
        name="sparse_up_both_ways",
        out_shape=(
            jax.ShapeDtypeStruct((tokens, CB * BLK), BF16),
            jax.ShapeDtypeStruct((SH, tokens), BF16),
            jax.ShapeDtypeStruct((CB, OWN, BLK, BLK), F32),
        ),
        in_specs=[smem, smem, vmem, vmem, pl.BlockSpec(memory_space=pl.ANY)],
        out_specs=(vmem, vmem, vmem),
        scratch_shapes=[
            pltpu.VMEM((NX, NY, NZ, NC, SH, BLK), BF16),
            pltpu.VMEM((CB, KB + 1, BLK, BLK), BF16),
            pltpu.VMEM((RB, BLK, BLK), BF16),
            pltpu.VMEM((CB, KB * BLK, BLK), BF16),
            pltpu.VMEM((BLK, CB * BLK), BF16),
            pltpu.VMEM((NX, NY, NZ, NC, SH, BLK), BF16),
            pltpu.VMEM((NX, NY, NZ, SH, BLK), BF16),
            pltpu.VMEM((NX - 1, NY, NZ, SH, BLK), BF16),
            pltpu.VMEM((NX - 1, NY, NZ, SH, BLK), BF16),
            pltpu.VMEM((NY, NZ, SH, BLK), F32),
            pltpu.VMEM((NZ, SH, BLK), BF16),
            pltpu.VMEM((NZ, SH, BLK), BF16),
            pltpu.VMEM((NZ, SH, BLK), F32),
            pltpu.VMEM((NZ, SH, BLK), BF16),
            pltpu.VMEM((NZ - 1, SH, BLK), BF16),
            pltpu.VMEM((2, *column), BF16),
            pltpu.VMEM((2, *column), BF16),
            pltpu.VMEM((2, CB, *column), BF16),
            pltpu.VMEM((2, CB, *column), BF16),
            pltpu.VMEM((2, *column), F32),
            dma,
            dma((NZ - 1,)), dma((NZ,)),
            dma((NB,)), dma((NB,)),
            dma((NX - 1, NY, NB)), dma((NX - 1, NY, NB)),
            dma((NX, NY, NB)), dma((NX, NY, NB)),
            dma((NX,)), dma((NX,)),
            dma((NX - 1, NY)), dma((NX - 1, NY)),
            dma, dma,
            dma((NZ - 1,)), dma((NZ - 1,)),
            dma((2,)), dma((2,)),
            dma((2, CB)), dma((2, CB)),
        ],
        compiler_params=pltpu.CompilerParams(
            collective_id=0, has_side_effects=True, vmem_limit_bytes=48 << 20
        ),
    )(block_rows, inverse, activations.T, cotangent, block_values)
    return gelu_out, dx.T, block_grad


def solution(mesh):
    in_specs = (P("mp", "dp"), P("dp", None, None, None), P("dp", None), P("mp", "dp"))
    out_specs = (P("mp", "dp"), P("mp", "dp"), P("dp", "mp", None, None))
    return jax.shard_map(body, mesh=mesh, in_specs=in_specs, out_specs=out_specs, check_vma=False)
```

time: 1330 us -> 86.3 us (0.06)
  waiting for transfers between devices: 1290 us -> 0 us
  Pallas kernels: 0 us -> 78.9 us
  between operations: 14.5 us -> 0.67 us
    reduce_scatter x1 -> x0, waiting for transfers between devices: 851 us -> none  [body(): lax.psum_scatter(dx_term, 'dp', scatter_dimension=1, tiled=True)]
    all_gather x1 -> x0, waiting for transfers between devices: 327 us -> none  [body(): x_full = lax.all_gather(activations, 'dp', axis=1, tiled=True)]
    unnamed x4 -> x0, waiting for transfers between devices: 107 us -> none
    pallas_call x0 -> x1, Pallas kernels: none -> 78.9 us  [body(): pl.pallas_call(kernel, name='sparse_up_both_ways', out_shape=(jax.ShapeDt...]
  transfers between devices with their start and end apart: 3 -> 0, of which waited for: 3 -> 0; matrix products, arithmetic and copies ran while one was open for 1% -> 0% of each run, Pallas kernels for 0% -> 0%
where the time goes in v1:
time: 86.3 us; the launch traced here: 86 us
  Pallas kernels  78.9 us (91%)
  local copies, waits for them, and re-layouts  6.37 us (7%)
    pallas_call x1, Pallas kernels, body(): pl.pallas_call(kernel, name='sparse_up_both_ways', out_shape=(jax.ShapeDt...  78.9 us
    unnamed x12, local copies, waits for them, and re-layouts  6.37 us

profile of v1, /device:TPU:1, one launch (start us, length us, event | category | flops | bytes accessed | tf_op | source)
XLA Modules:
  0.0 86.0 jit_solution(18086174336087646004)
XLA Ops:
  0.6 0.8 copy.7
  1.4 0.1 fusion
  1.5 0.0 copy-start
  1.6 1.3 %copy-done = bf16[2,20,128,128]{3,2,1,0:T(8,128)(2,1)S(1)} copy-done((bf16[2,20,128,128]{3,2,1,0:T(8,128)(2,1)S(1)}, bf16[2,20,128,128]{3,2,1,0:T(8,128)(2,1)}, u32[]{:S(2)}) %copy-start) | copy-done | bytes 1310744
  2.9 0.0 copy-start.1
  2.9 0.8 copy-done.1
  3.7 0.0 copy-start.2
  3.7 0.7 copy-done.2
  4.4 0.0 copy-start.3
  4.4 0.7 copy-done.3
  5.1 78.9 %sparse_up_both_ways.1 = (bf16[128,256]{1,0:T(8,128)(2,1)S(1)}, bf16[48,128]{1,0:T(8,128)(2,1)S(1)}, f32[2,5,128,128]{3,2,1,0:T(8,128)S(1)}) custom-call(s32[2,20]{1,0:T(2,128)S(1)} %copy-done.3, s32[2,72]{1,0:T(2,128)S(1)} %broadcast_add_fusion.inv_ref, bf16[48,128]{1,0:T(8,128)(2,1)S(1)} %bitcast.2, bf16[128,256]{1,0:T(8,128)(2,1)S(1)} %copy-done.1, ...), custom_call_target="tpu_custom_call" | custom-call | tf_op jit(solution)/shard_map/sparse_up_both_ways/pallas_call | solution.py:249
  84.0 0.6 copy.11
  84.6 0.6 copy.12
  85.2 0.8 copy.13
  (2 shorter events, 0.0 us)
Async XLA Ops:
  1.5 1.3 %copy-start = (bf16[2,20,128,128]{3,2,1,0:T(8,128)(2,1)S(1)}, bf16[2,20,128,128]{3,2,1,0:T(8,128)(2,1)}, u32[]{:S(2)}) copy-start(bf16[2,20,128,128]{3,2,1,0:T(8,128)(2,1)} %w_hbm.1) | copy-start | bytes 3932164
  2.9 0.8 copy-start.1
  3.7 0.7 copy-start.2
  4.4 0.7 copy-start.3

commit v2 on v1

v2 whole, which is shorter than its diff:
```python
import functools

import jax
import jax.numpy as jnp
from jax import lax
from jax.experimental import pallas as pl
from jax.experimental.pallas import tpu as pltpu
from jax.sharding import PartitionSpec as P

NX, NY, NZ, NC, NM = 4, 2, 12, 2, 4
BLK, KB, RB, CB = 128, 20, 72, 2
SH = 48
ZB = 4
RANK = (0, 1, 11, 2, 10, 3, 9, 4, 8, 5, 7, 6)
GROUPS = ((0, 1), (1, 2), (3, 4), (7, 5))
NG = len(GROUPS)
X_FIRST = (2,)
OWN = KB // NM
FAR_FIRST = (2, 1, 3)
F32, BF16 = jnp.float32, jnp.bfloat16
C0 = 0.7978845608028654
C1 = 0.044715


def coords():
    d = lax.axis_index("dp")
    c = lax.rem(d, NC)
    z = lax.rem(lax.div(d, NC), NZ)
    y = lax.rem(lax.div(d, NC * NZ), NY)
    x = lax.div(d, NC * NZ * NY)
    return x, y, z, c, lax.axis_index("mp")


def device(x, y, z, c, m):
    return (((x * NY + y) * NZ + z) * NC + c, m)


def remote(src, dst, send, recv, to):
    return pltpu.make_async_remote_copy(
        src_ref=src, dst_ref=dst, send_sem=send, recv_sem=recv,
        device_id=to, device_id_type=pl.DeviceIdType.MESH,
    )


def kernel(
    rows_hbm, xt_hbm, cot_hbm, w_hbm,
    gelu_ref, dx_ref, bg_ref,
    X, W, COT, XQ, XF, XP, SL, D, S, XS, XR, OX, YS, YR, ZR0, ZS, ZR,
    GS1, GR1, GS2, GR2, GP, IV, ROWS, INV,
    isem, zs, zr, ys, yr, xs, xr, bs, br,
    ss, sr, rxs, rxr, rys, ryr, rzs, rzr, g1s, g1r, g2s, g2r,
):
    x, y, z, c, m = coords()
    oy, oc = 1 - y, 1 - c
    side = (y, oy)
    xa = [x] + [lax.rem(x + j, NX) for j in range(1, NX)]
    za = [z] + [lax.rem(z + k, NZ) for k in range(1, NZ)]
    m1, m2, m3 = (lax.rem(m + k, NM) for k in (1, 2, 3))
    to_x = [None] + [device(xa[j], y, z, c, m) for j in range(1, NX)]
    to_z = [None] + [device(x, y, za[k], c, m) for k in range(1, NZ)]
    to_y = device(x, oy, z, c, m)
    to_c = device(x, y, z, oc, m)
    to_up, to_down = device(x, y, z, c, m1), device(x, y, z, c, m3)

    own_x = pltpu.make_async_copy(xt_hbm, X.at[0, 0, 0, 0], isem.at[0])
    rows_in = pltpu.make_async_copy(rows_hbm, ROWS, isem.at[1])
    w_in = pltpu.make_async_copy(w_hbm, W.at[:, pl.ds(0, KB)], isem.at[2])
    cot_in = pltpu.make_async_copy(cot_hbm, COT, isem.at[3])
    for copy in (own_x, rows_in, w_in, cot_in):
        copy.start()

    barrier = pltpu.get_barrier_semaphore()
    partners = to_z[1:] + to_x[1:] + [to_y, to_c, to_up, to_down]
    for d in partners:
        pl.semaphore_signal(barrier, inc=1, device_id=d, device_id_type=pl.DeviceIdType.MESH)
    own_x.wait()
    pl.semaphore_wait(barrier, len(partners))

    started = []

    def go(copy):
        copy.start()
        started.append(copy)

    def drain():
        for copy in started:
            copy.wait_send()
        started.clear()

    def ranks(i):
        return range(GROUPS[i][0], sum(GROUPS[i]))

    def part(j, p, i, cc=0):
        return X.at[j, p, pl.ds(*GROUPS[i]), cc]

    def z_in(n, to):
        back = RANK.index((NZ - RANK[n]) % NZ)
        return remote(X.at[0, 0, 0, 0], X.at[0, 0, back, 0], zs.at[back], zr.at[back], to)

    def x_in(j, p, i):
        return remote(part(0, p, i), part(j, p, i), xs.at[j - 1, p, i], xr.at[j - 1, p, i], to_x[j])

    def y_in(j, i):
        return remote(part(j, 0, i), part(j, 1, i), ys.at[j, i], yr.at[j, i], to_y)

    def c_in(j, p, i):
        return remote(part(j, p, i), part(j, p, i, 1), bs.at[j, p, i], br.at[j, p, i], to_c)

    def send_x(p, i):
        for j in FAR_FIRST:
            go(x_in(j, p, i))

    def y_then_x(i):
        y_in(0, i).wait_recv()
        send_x(1, i)
        go(c_in(0, 1, i))

    def x_then_y(i):
        for j in (1, 3, 2):
            x_in(j, 0, i).wait_recv()
            go(y_in(j, i))
            go(c_in(j, 0, i))

    for n in range(1, NZ):
        go(z_in(n, to_z[RANK[n]]))
    waiting = []
    for i in range(NG):
        for n in ranks(i):
            if n:
                z_in(RANK.index((NZ - RANK[n]) % NZ), to_y).wait_recv()
        go(y_in(0, i))
        send_x(0, i)
        go(c_in(0, 0, i))
        if waiting:
            waiting.pop(0)()
        waiting.append(functools.partial(x_then_y if i in X_FIRST else y_then_x, i))
    for step in waiting:
        step()

    rows_in.wait()
    lanes = lax.broadcasted_iota(jnp.int32, (1, BLK), 1)
    for cb in range(CB):
        found = jnp.full((1, BLK), KB, jnp.int32)
        for k in range(KB):
            found = jnp.where(lanes == ROWS[cb, k], k, found)
        IV[pl.ds(cb, 1)] = found
    inv_in = pltpu.make_async_copy(IV, INV, isem.at[1])
    inv_in.start()
    w_in.wait()
    cot_in.wait()
    for cb in range(CB):
        W[cb, KB] = jnp.zeros((BLK, BLK), BF16)
    inv_in.wait()

    for i in range(NG):
        for j in (1, 3, 2):
            for p in range(NY):
                if i not in X_FIRST:
                    x_in(j, p, i).wait_recv()
                    go(c_in(j, p, i))
    for i in X_FIRST:
        for j in (0, 1, 3, 2):
            y_in(j, i).wait_recv()
            go(c_in(j, 1, i))
    for i in range(NG):
        for j in (0, 1, 3, 2):
            for p in range(NY):
                c_in(j, p, i).wait_recv()

    for j in range(NX):
        for p in range(NY):
            for n in range(NZ):
                XQ[xa[(NX - j) % NX], side[p], za[RANK[n]], c] = X[j, p, n, 0]
                XQ[xa[(NX - j) % NX], side[p], za[RANK[n]], oc] = X[j, p, n, 1]
    XF[...] = XQ[...].reshape(RB, BLK, BLK)
    for cb in range(CB):
        for k in range(KB):
            XP[cb, pl.ds(k * BLK, BLK)] = XF[ROWS[cb, k]]
    for cb in range(CB):
        cols = pl.ds(cb * BLK, BLK)
        v = lax.dot_general(
            XP[cb], W[cb, :KB].reshape(KB * BLK, BLK), (((0,), (0,)), ((), ())),
            preferred_element_type=F32,
        )
        t = jnp.tanh(C0 * (v + C1 * (v * v * v)))
        gelu_ref[:, cols] = (0.5 * v * (1.0 + t)).astype(BF16)
        slope = 0.5 * (1.0 + t) + 0.5 * v * (1.0 - t * t) * (C0 * (1.0 + 3.0 * C1 * (v * v)))
        SL[:, cols] = (COT[:, cols].astype(F32) * slope).astype(BF16)

    def grads(cb, group):
        return jnp.dot(
            XP[cb, pl.ds(group * (OWN * BLK), OWN * BLK)], SL[:, cb * BLK : (cb + 1) * BLK],
            preferred_element_type=F32,
        )

    def g1(cb, to):
        return remote(GS1.at[cb], GR1.at[cb], g1s.at[cb], g1r.at[cb], to)

    def g2(way, cb, to):
        return remote(GS2.at[way, cb], GR2.at[way, cb], g2s.at[way, cb], g2r.at[way, cb], to)

    GS1[0] = grads(0, m2).astype(BF16)
    go(g1(0, to_up))
    GS1[1] = grads(1, m2).astype(BF16)
    go(g1(1, to_down))

    def pair_copy(j, p):
        return remote(D.at[xa[j], side[p], :, oc], S.at[j, p], ss.at[j, p], sr.at[j, p], to_c)

    def terms(j, p):
        first = xa[j] * (RB // NX) + side[p] * (RB // NX // NY)

        def step(g, carry):
            made = []
            for n in range(3):
                r = first + g * 3 + n
                pair = jnp.concatenate([W[0, INV[0, r]], W[1, INV[1, r]]], axis=1)
                made.append(
                    lax.dot_general(pair, SL[...], (((1,), (1,)), ((), ())), preferred_element_type=F32)
                )
            both = jnp.concatenate(made, axis=0).reshape(ZB, NC, SH, BLK).astype(BF16)
            D[xa[j], side[p], pl.ds(g * ZB, ZB)] = both
            return carry

        lax.fori_loop(0, NZ // ZB, step, 0)
        go(pair_copy(j, p))

    def both_cores(j, p, n):
        zz = za[RANK[n]]
        return D[xa[j], side[p], zz, c].astype(F32) + S[j, p, zz].astype(F32)

    def x_copy(j, p, i):
        at = pl.ds(*GROUPS[i])
        return remote(
            XS.at[j - 1, p, at], XR.at[j - 1, p, at], rxs.at[j - 1, p, i], rxr.at[j - 1, p, i], to_x[j]
        )

    def y_copy(i):
        at = pl.ds(*GROUPS[i])
        return remote(YS.at[at], YR.at[at], rys.at[i], ryr.at[i], to_y)

    def z_copy(n, to):
        back = RANK.index((NZ - RANK[n]) % NZ)
        return remote(ZS.at[n], ZR.at[back], rzs.at[n], rzr.at[back], to)

    def second(way, cb, to):
        g1(cb, to).wait_recv()
        GS2[way, cb] = (GP[cb] + GR1[cb].astype(F32)).astype(BF16)
        go(g2(way, cb, to))

    far_groups = range(NG - 1, -1, -1)

    def along_x(p, i):
        for j in FAR_FIRST:
            for n in ranks(i):
                XS[j - 1, p, n] = both_cores(j, p, n).astype(BF16)
            go(x_copy(j, p, i))

    for p in (1, 0):
        for j in (2, 1, 3, 0):
            terms(j, p)
    for p in (1, 0):
        for j in FAR_FIRST:
            pair_copy(j, p).wait_recv()
        for i in far_groups:
            if p == 1:
                along_x(1, i)
    for i in far_groups:
        along_x(0, i)
    GS2[0, 1] = grads(1, m1).astype(BF16)
    go(g2(0, 1, to_up))
    GS2[1, 0] = grads(0, m3).astype(BF16)
    go(g2(1, 0, to_down))
    for p in (1, 0):
        pair_copy(0, p).wait_recv()
        for n in range(NZ):
            OX[p, n] = both_cores(0, p, n)
    GP[0] = grads(0, m1)
    GP[1] = grads(1, m3)
    for cb in range(CB):
        bg_ref[cb] = grads(cb, m).reshape(OWN, BLK, BLK)

    def from_x(p, i):
        at = pl.ds(*GROUPS[i])
        total = OX[p, at]
        for j in FAR_FIRST:
            x_copy(j, p, i).wait_recv()
            total = total + XR[j - 1, p, at].astype(F32)
        return total

    for i in far_groups:
        YS[pl.ds(*GROUPS[i])] = from_x(1, i).astype(BF16)
        go(y_copy(i))
    for i in far_groups:
        at = pl.ds(*GROUPS[i])
        total = from_x(0, i)
        y_copy(i).wait_recv()
        total = total + YR[at].astype(F32)
        if i == 0:
            ZR0[...] = total
            continue
        ZS[at] = total.astype(BF16)
        for n in ranks(i):
            go(z_copy(n, to_z[RANK[n]]))
        if i == NG - 1:
            second(0, 0, to_up)
            second(1, 1, to_down)
    dx = ZR0[0]

    def add(way, cb):
        g2(way, cb, to_up).wait_recv()
        bg_ref[cb] = bg_ref[cb] + GR2[way, cb].astype(F32).reshape(OWN, BLK, BLK)

    for n in range(1, NZ):
        z_copy(RANK.index((NZ - RANK[n]) % NZ), to_y).wait_recv()
        dx = dx + ZR[n].astype(F32)
    dx_ref[...] = dx.astype(BF16)
    add(0, 1)
    add(1, 0)
    add(0, 0)
    add(1, 1)
    drain()


def body(activations, block_values, block_rows, cotangent):
    tokens = activations.shape[0]
    hbm, vmem = pl.BlockSpec(memory_space=pltpu.HBM), pl.BlockSpec(memory_space=pltpu.VMEM)
    dma = pltpu.SemaphoreType.DMA
    column = (OWN * BLK, BLK)
    gelu_out, dx, block_grad = pl.pallas_call(
        kernel,
        name="sparse_up_both_ways",
        out_shape=(
            jax.ShapeDtypeStruct((tokens, CB * BLK), BF16),
            jax.ShapeDtypeStruct((SH, tokens), BF16),
            jax.ShapeDtypeStruct((CB, OWN, BLK, BLK), F32),
        ),
        in_specs=[hbm] * 4,
        out_specs=(vmem, vmem, vmem),
        scratch_shapes=[
            pltpu.VMEM((NX, NY, NZ, NC, SH, BLK), BF16),
            pltpu.VMEM((CB, KB + 1, BLK, BLK), BF16),
            pltpu.VMEM((BLK, CB * BLK), BF16),
            pltpu.VMEM((NX, NY, NZ, NC, SH, BLK), BF16),
            pltpu.VMEM((RB, BLK, BLK), BF16),
            pltpu.VMEM((CB, KB * BLK, BLK), BF16),
            pltpu.VMEM((BLK, CB * BLK), BF16),
            pltpu.VMEM((NX, NY, NZ, NC, SH, BLK), BF16),
            pltpu.VMEM((NX, NY, NZ, SH, BLK), BF16),
            pltpu.VMEM((NX - 1, NY, NZ, SH, BLK), BF16),
            pltpu.VMEM((NX - 1, NY, NZ, SH, BLK), BF16),
            pltpu.VMEM((NY, NZ, SH, BLK), F32),
            pltpu.VMEM((NZ, SH, BLK), BF16),
            pltpu.VMEM((NZ, SH, BLK), BF16),
            pltpu.VMEM((1, SH, BLK), F32),
            pltpu.VMEM((NZ, SH, BLK), BF16),
            pltpu.VMEM((NZ, SH, BLK), BF16),
            pltpu.VMEM((2, *column), BF16),
            pltpu.VMEM((2, *column), BF16),
            pltpu.VMEM((2, CB, *column), BF16),
            pltpu.VMEM((2, CB, *column), BF16),
            pltpu.VMEM((2, *column), F32),
            pltpu.VMEM((CB, BLK), jnp.int32),
            pltpu.SMEM((CB, KB), jnp.int32),
            pltpu.SMEM((CB, BLK), jnp.int32),
            dma((4,)),
            dma((NZ,)), dma((NZ,)),
            dma((NX, NG)), dma((NX, NG)),
            dma((NX - 1, NY, NG)), dma((NX - 1, NY, NG)),
            dma((NX, NY, NG)), dma((NX, NY, NG)),
            dma((NX, NY)), dma((NX, NY)),
            dma((NX - 1, NY, NG)), dma((NX - 1, NY, NG)),
            dma((NG,)), dma((NG,)),
            dma((NZ,)), dma((NZ,)),
            dma((2,)), dma((2,)),
            dma((2, CB)), dma((2, CB)),
        ],
        compiler_params=pltpu.CompilerParams(
            collective_id=0, has_side_effects=True, vmem_limit_bytes=48 << 20
        ),
    )(block_rows, activations.T, cotangent, block_values)
    return gelu_out, dx.T, block_grad


def solution(mesh):
    in_specs = (P("mp", "dp"), P("dp", None, None, None), P("dp", None), P("mp", "dp"))
    out_specs = (P("mp", "dp"), P("mp", "dp"), P("dp", "mp", None, None))
    return jax.shard_map(body, mesh=mesh, in_specs=in_specs, out_specs=out_specs, check_vma=False)
```

time: 86.3 us -> 75.7 us (0.88)
  Pallas kernels: 78.9 us -> 69.2 us
    pallas_call x1, Pallas kernels: 78.9 us -> 69.2 us  [body(): pl.pallas_call(kernel, name='sparse_up_both_ways', out_shape=(jax.ShapeDt...]
    unnamed x12 -> x11, local copies, waits for them, and re-layouts: 6.37 us -> 5.6 us
where the time goes in v2:
time: 75.7 us; the launch traced here: 75.4 us
  Pallas kernels  69.2 us (91%)
  local copies, waits for them, and re-layouts  5.6 us (7%)
    pallas_call x1, Pallas kernels, body(): pl.pallas_call(kernel, name='sparse_up_both_ways', out_shape=(jax.ShapeDt...  69.2 us
    unnamed x11, local copies, waits for them, and re-layouts  5.6 us

profile of v2, /device:TPU:1, one launch (start us, length us, event | category | flops | bytes accessed | tf_op | source)
XLA Modules:
  0.0 75.4 jit_solution(17443777419342572314)
XLA Ops:
  0.6 0.0 copy-start
  0.6 1.3 %copy-done = bf16[2,20,128,128]{3,2,1,0:T(8,128)(2,1)S(1)} copy-done((bf16[2,20,128,128]{3,2,1,0:T(8,128)(2,1)S(1)}, bf16[2,20,128,128]{3,2,1,0:T(8,128)(2,1)}, u32[]{:S(2)}) %copy-start) | copy-done | bytes 1310744
  1.9 0.0 copy-start.1
  2.0 0.8 %copy-done.1 = bf16[128,256]{1,0:T(8,128)(2,1)S(1)} copy-done((bf16[128,256]{1,0:T(8,128)(2,1)S(1)}, bf16[128,256]{1,0:T(8,128)(2,1)}, u32[]{:S(2)}) %copy-start.1) | copy-done | bytes 65560
  2.8 0.0 copy-start.2
  2.8 0.7 copy-done.2
  3.5 0.0 copy-start.3
  3.5 0.7 copy-done.3
  4.2 69.2 %sparse_up_both_ways.1 = (bf16[128,256]{1,0:T(8,128)(2,1)S(1)}, bf16[48,128]{1,0:T(8,128)(2,1)S(1)}, f32[2,5,128,128]{3,2,1,0:T(8,128)S(1)}) custom-call(s32[2,20]{1,0:T(2,128)S(1)} %copy-done.3, bf16[48,128]{1,0:T(8,128)(2,1)S(1)} %bitcast.2, bf16[128,256]{1,0:T(8,128)(2,1)S(1)} %copy-done.1, bf16[2,20,128,128]{3,2,1,0:T(8,128)(2,1)S(1)} %copy-done), custom_call_target="tpu_custom_call" | custom-call | tf_op jit(solution)/shard_map/sparse_up_both_ways/pallas_call | solution.py:330
  73.3 0.6 copy.10
  74.0 0.6 copy.11
  74.6 0.8 %copy.12 = f32[2,5,128,128]{3,2,1,0:T(8,128)} copy(f32[2,5,128,128]{3,2,1,0:T(8,128)S(1)} %get-tuple-element.14) | data formatting | bytes 1310720
Async XLA Ops:
  0.6 1.3 %copy-start = (bf16[2,20,128,128]{3,2,1,0:T(8,128)(2,1)S(1)}, bf16[2,20,128,128]{3,2,1,0:T(8,128)(2,1)}, u32[]{:S(2)}) copy-start(bf16[2,20,128,128]{3,2,1,0:T(8,128)(2,1)} %w_hbm.1) | copy-start | bytes 3932164
  1.9 0.8 %copy-start.1 = (bf16[128,256]{1,0:T(8,128)(2,1)S(1)}, bf16[128,256]{1,0:T(8,128)(2,1)}, u32[]{:S(2)}) copy-start(bf16[128,256]{1,0:T(8,128)(2,1)} %cot_hbm.1) | copy-start | bytes 196612
  2.8 0.7 copy-start.2
  3.5 0.7 copy-start.3

commit v3 on v2

--- a/solution.py
+++ b/solution.py
@@ -14,7 +14,6 @@
 RANK = (0, 1, 11, 2, 10, 3, 9, 4, 8, 5, 7, 6)
 GROUPS = ((0, 1), (1, 2), (3, 4), (7, 5))
 NG = len(GROUPS)
-X_FIRST = (2,)
 OWN = KB // NM
 FAR_FIRST = (2, 1, 3)
 F32, BF16 = jnp.float32, jnp.bfloat16
@@ -45,7 +44,7 @@
 def kernel(
     rows_hbm, xt_hbm, cot_hbm, w_hbm,
     gelu_ref, dx_ref, bg_ref,
-    X, W, COT, XQ, XF, XP, SL, D, S, XS, XR, OX, YS, YR, ZR0, ZS, ZR,
+    X, W, COT, XQ, XF, XP, SL, SLT, D, S, XS, XR, OX, YS, YR, ZR0, ZS, ZR,
     GS1, GR1, GS2, GR2, GP, IV, ROWS, INV,
     isem, zs, zr, ys, yr, xs, xr, bs, br,
     ss, sr, rxs, rxr, rys, ryr, rzs, rzr, g1s, g1r, g2s, g2r,
@@ -123,19 +122,31 @@
 
     for n in range(1, NZ):
         go(z_in(n, to_z[RANK[n]]))
-    waiting = []
-    for i in range(NG):
+    def along_z(i):
         for n in ranks(i):
             if n:
                 z_in(RANK.index((NZ - RANK[n]) % NZ), to_y).wait_recv()
         go(y_in(0, i))
         send_x(0, i)
         go(c_in(0, 0, i))
-        if waiting:
-            waiting.pop(0)()
-        waiting.append(functools.partial(x_then_y if i in X_FIRST else y_then_x, i))
-    for step in waiting:
-        step()
+
+    def x_to_core(p, i):
+        for j in (1, 3, 2):
+            x_in(j, p, i).wait_recv()
+            go(c_in(j, p, i))
+
+    along_z(0)
+    along_z(1)
+    y_then_x(0)
+    along_z(2)
+    y_then_x(1)
+    x_to_core(0, 0)
+    x_to_core(1, 0)
+    x_to_core(0, 1)
+    along_z(3)
+    x_then_y(2)
+    y_then_x(3)
+    x_to_core(1, 1)
 
     rows_in.wait()
     lanes = lax.broadcasted_iota(jnp.int32, (1, BLK), 1)
@@ -152,16 +163,11 @@
         W[cb, KB] = jnp.zeros((BLK, BLK), BF16)
     inv_in.wait()
 
-    for i in range(NG):
-        for j in (1, 3, 2):
-            for p in range(NY):
-                if i not in X_FIRST:
-                    x_in(j, p, i).wait_recv()
-                    go(c_in(j, p, i))
-    for i in X_FIRST:
-        for j in (0, 1, 3, 2):
-            y_in(j, i).wait_recv()
-            go(c_in(j, 1, i))
+    for j in (0, 1, 3, 2):
+        y_in(j, 2).wait_recv()
+        go(c_in(j, 1, 2))
+    x_to_core(0, 3)
+    x_to_core(1, 3)
     for i in range(NG):
         for j in (0, 1, 3, 2):
             for p in range(NY):
@@ -204,6 +210,12 @@
     GS1[1] = grads(1, m2).astype(BF16)
     go(g1(1, to_down))
 
+    GS2[0, 1] = grads(1, m1).astype(BF16)
+    go(g2(0, 1, to_up))
+    GS2[1, 0] = grads(0, m3).astype(BF16)
+    go(g2(1, 0, to_down))
+    SLT[...] = SL[...].T
+
     def pair_copy(j, p):
         return remote(D.at[xa[j], side[p], :, oc], S.at[j, p], ss.at[j, p], sr.at[j, p], to_c)
 
@@ -211,15 +223,10 @@
         first = xa[j] * (RB // NX) + side[p] * (RB // NX // NY)
 
         def step(g, carry):
-            made = []
-            for n in range(3):
-                r = first + g * 3 + n
-                pair = jnp.concatenate([W[0, INV[0, r]], W[1, INV[1, r]]], axis=1)
-                made.append(
-                    lax.dot_general(pair, SL[...], (((1,), (1,)), ((), ())), preferred_element_type=F32)
-                )
-            both = jnp.concatenate(made, axis=0).reshape(ZB, NC, SH, BLK).astype(BF16)
-            D[xa[j], side[p], pl.ds(g * ZB, ZB)] = both
+            picks = [(INV[0, first + g * 3 + n], INV[1, first + g * 3 + n]) for n in range(3)]
+            halves = [jnp.concatenate([W[cb, k[cb]] for k in picks], axis=0) for cb in range(CB)]
+            made = jnp.dot(jnp.concatenate(halves, axis=1), SLT[...], preferred_element_type=F32)
+            D[xa[j], side[p], pl.ds(g * ZB, ZB)] = made.reshape(ZB, NC, SH, BLK).astype(BF16)
             return carry
 
         lax.fori_loop(0, NZ // ZB, step, 0)
@@ -267,10 +274,6 @@
                 along_x(1, i)
     for i in far_groups:
         along_x(0, i)
-    GS2[0, 1] = grads(1, m1).astype(BF16)
-    go(g2(0, 1, to_up))
-    GS2[1, 0] = grads(0, m3).astype(BF16)
-    go(g2(1, 0, to_down))
     for p in (1, 0):
         pair_copy(0, p).wait_recv()
         for n in range(NZ):
@@ -345,6 +348,7 @@
             pltpu.VMEM((RB, BLK, BLK), BF16),
             pltpu.VMEM((CB, KB * BLK, BLK), BF16),
             pltpu.VMEM((BLK, CB * BLK), BF16),
+            pltpu.VMEM((CB * BLK, BLK), BF16),
             pltpu.VMEM((NX, NY, NZ, NC, SH, BLK), BF16),
             pltpu.VMEM((NX, NY, NZ, SH, BLK), BF16),
             pltpu.VMEM((NX - 1, NY, NZ, SH, BLK), BF16),
@@ -376,7 +380,7 @@
             dma((2, CB)), dma((2, CB)),
         ],
         compiler_params=pltpu.CompilerParams(
-            collective_id=0, has_side_effects=True, vmem_limit_bytes=48 << 20
+            collective_id=0, has_side_effects=True, vmem_limit_bytes=52 << 20
         ),
     )(block_rows, activations.T, cotangent, block_values)
     return gelu_out, dx.T, block_grad

time: 75.7 us -> 72.8 us (0.962); the launches traced: 75.4 us -> 71.6 us
  Pallas kernels: 69.2 us -> 66.7 us
  local copies, waits for them, and re-layouts: 5.6 us -> 4.28 us
    pallas_call x1, Pallas kernels: 69.2 us -> 66.7 us  [body(): pl.pallas_call(kernel, name='sparse_up_both_ways', out_shape=(jax.ShapeDt...]
    unnamed x11 -> x9, local copies, waits for them, and re-layouts: 5.6 us -> 4.28 us
where the time goes in v3:
time: 72.8 us; the launch traced here: 71.6 us
  Pallas kernels  66.7 us (92%)
  local copies, waits for them, and re-layouts  4.28 us (6%)
    pallas_call x1, Pallas kernels, body(): pl.pallas_call(kernel, name='sparse_up_both_ways', out_shape=(jax.ShapeDt...  66.7 us
    unnamed x9, local copies, waits for them, and re-layouts  4.28 us

profile of v3, /device:TPU:1, one launch (start us, length us, event | category | flops | bytes accessed | tf_op | source)
XLA Modules:
  0.0 71.6 jit_solution(13354524004704770758)
XLA Ops:
  0.6 0.0 copy-start
  0.6 0.8 %copy-done = bf16[128,256]{1,0:T(8,128)(2,1)S(1)} copy-done((bf16[128,256]{1,0:T(8,128)(2,1)S(1)}, bf16[128,256]{1,0:T(8,128)(2,1)}, u32[]{:S(2)}) %copy-start) | copy-done | bytes 65560
  1.5 0.0 copy-start.1
  1.5 0.7 copy-done.1
  2.2 0.0 copy-start.2
  2.2 0.7 copy-done.2
  2.9 66.7 %sparse_up_both_ways.1 = (bf16[128,256]{1,0:T(8,128)(2,1)S(1)}, bf16[48,128]{1,0:T(8,128)(2,1)S(1)}, f32[2,5,128,128]{3,2,1,0:T(8,128)S(1)}) custom-call(s32[2,20]{1,0:T(2,128)S(1)} %copy-done.2, bf16[48,128]{1,0:T(8,128)(2,1)S(1)} %bitcast.2, bf16[128,256]{1,0:T(8,128)(2,1)S(1)} %copy-done, bf16[2,20,128,128]{3,2,1,0:T(8,128)(2,1)} %w_hbm.1), custom_call_target="tpu_custom_call" | custom-call | tf_op jit(solution)/shard_map/sparse_up_both_ways/pallas_call | solution.py:333
  69.5 0.6 copy.10
  70.2 0.6 copy.11
  70.8 0.8 %copy.12 = f32[2,5,128,128]{3,2,1,0:T(8,128)} copy(f32[2,5,128,128]{3,2,1,0:T(8,128)S(1)} %get-tuple-element.14) | data formatting | bytes 1310720
Async XLA Ops:
  0.6 0.8 %copy-start = (bf16[128,256]{1,0:T(8,128)(2,1)S(1)}, bf16[128,256]{1,0:T(8,128)(2,1)}, u32[]{:S(2)}) copy-start(bf16[128,256]{1,0:T(8,128)(2,1)} %cot_hbm.1) | copy-start | bytes 196612
  1.5 0.7 copy-start.1
  2.2 0.7 copy-start.2

commit v4 on v3

--- a/solution.py
+++ b/solution.py
@@ -14,6 +14,8 @@
 RANK = (0, 1, 11, 2, 10, 3, 9, 4, 8, 5, 7, 6)
 GROUPS = ((0, 1), (1, 2), (3, 4), (7, 5))
 NG = len(GROUPS)
+SUM_GROUPS = ((0, 1), (1, 6), (7, 5))
+NS = len(SUM_GROUPS)
 OWN = KB // NM
 FAR_FIRST = (2, 1, 3)
 F32, BF16 = jnp.float32, jnp.bfloat16
@@ -232,18 +234,21 @@
         lax.fori_loop(0, NZ // ZB, step, 0)
         go(pair_copy(j, p))
 
+    def sum_ranks(i):
+        return range(SUM_GROUPS[i][0], sum(SUM_GROUPS[i]))
+
     def both_cores(j, p, n):
         zz = za[RANK[n]]
         return D[xa[j], side[p], zz, c].astype(F32) + S[j, p, zz].astype(F32)
 
     def x_copy(j, p, i):
-        at = pl.ds(*GROUPS[i])
+        at = pl.ds(*SUM_GROUPS[i])
         return remote(
             XS.at[j - 1, p, at], XR.at[j - 1, p, at], rxs.at[j - 1, p, i], rxr.at[j - 1, p, i], to_x[j]
         )
 
     def y_copy(i):
-        at = pl.ds(*GROUPS[i])
+        at = pl.ds(*SUM_GROUPS[i])
         return remote(YS.at[at], YR.at[at], rys.at[i], ryr.at[i], to_y)
 
     def z_copy(n, to):
@@ -255,11 +260,11 @@
         GS2[way, cb] = (GP[cb] + GR1[cb].astype(F32)).astype(BF16)
         go(g2(way, cb, to))
 
-    far_groups = range(NG - 1, -1, -1)
+    far_groups = range(NS - 1, -1, -1)
 
     def along_x(p, i):
         for j in FAR_FIRST:
-            for n in ranks(i):
+            for n in sum_ranks(i):
                 XS[j - 1, p, n] = both_cores(j, p, n).astype(BF16)
             go(x_copy(j, p, i))
 
@@ -284,7 +289,7 @@
         bg_ref[cb] = grads(cb, m).reshape(OWN, BLK, BLK)
 
     def from_x(p, i):
-        at = pl.ds(*GROUPS[i])
+        at = pl.ds(*SUM_GROUPS[i])
         total = OX[p, at]
         for j in FAR_FIRST:
             x_copy(j, p, i).wait_recv()
@@ -292,10 +297,10 @@
         return total
 
     for i in far_groups:
-        YS[pl.ds(*GROUPS[i])] = from_x(1, i).astype(BF16)
+        YS[pl.ds(*SUM_GROUPS[i])] = from_x(1, i).astype(BF16)
         go(y_copy(i))
     for i in far_groups:
-        at = pl.ds(*GROUPS[i])
+        at = pl.ds(*SUM_GROUPS[i])
         total = from_x(0, i)
         y_copy(i).wait_recv()
         total = total + YR[at].astype(F32)
@@ -303,9 +308,9 @@
             ZR0[...] = total
             continue
         ZS[at] = total.astype(BF16)
-        for n in ranks(i):
+        for n in sum_ranks(i):
             go(z_copy(n, to_z[RANK[n]]))
-        if i == NG - 1:
+        if i == NS - 1:
             second(0, 0, to_up)
             second(1, 1, to_down)
     dx = ZR0[0]
@@ -373,8 +378,8 @@
             dma((NX - 1, NY, NG)), dma((NX - 1, NY, NG)),
             dma((NX, NY, NG)), dma((NX, NY, NG)),
             dma((NX, NY)), dma((NX, NY)),
-            dma((NX - 1, NY, NG)), dma((NX - 1, NY, NG)),
-            dma((NG,)), dma((NG,)),
+            dma((NX - 1, NY, NS)), dma((NX - 1, NY, NS)),
+            dma((NS,)), dma((NS,)),
             dma((NZ,)), dma((NZ,)),
             dma((2,)), dma((2,)),
             dma((2, CB)), dma((2, CB)),

time: 72.8 us -> 72.7 us (level)
  no operation moved by 1% of the time
where the time goes in v4:
time: 72.7 us; the launch traced here: 71.8 us
  Pallas kernels  66.8 us (92%)
  local copies, waits for them, and re-layouts  4.28 us (6%)
    pallas_call x1, Pallas kernels, body(): pl.pallas_call(kernel, name='sparse_up_both_ways', out_shape=(jax.ShapeDt...  66.8 us
    unnamed x9, local copies, waits for them, and re-layouts  4.28 us

profile of v4, /device:TPU:1, one launch (start us, length us, event | category | flops | bytes accessed | tf_op | source)
XLA Modules:
  0.0 71.8 jit_solution(13940350164059681570)
XLA Ops:
  0.6 0.0 copy-start
  0.6 0.8 %copy-done = bf16[128,256]{1,0:T(8,128)(2,1)S(1)} copy-done((bf16[128,256]{1,0:T(8,128)(2,1)S(1)}, bf16[128,256]{1,0:T(8,128)(2,1)}, u32[]{:S(2)}) %copy-start) | copy-done | bytes 65560
  1.5 0.0 copy-start.1
  1.5 0.7 copy-done.1
  2.2 0.0 copy-start.2
  2.2 0.7 copy-done.2
  2.9 66.8 %sparse_up_both_ways.1 = (bf16[128,256]{1,0:T(8,128)(2,1)S(1)}, bf16[48,128]{1,0:T(8,128)(2,1)S(1)}, f32[2,5,128,128]{3,2,1,0:T(8,128)S(1)}) custom-call(s32[2,20]{1,0:T(2,128)S(1)} %copy-done.2, bf16[48,128]{1,0:T(8,128)(2,1)S(1)} %bitcast.2, bf16[128,256]{1,0:T(8,128)(2,1)S(1)} %copy-done, bf16[2,20,128,128]{3,2,1,0:T(8,128)(2,1)} %w_hbm.1), custom_call_target="tpu_custom_call" | custom-call | tf_op jit(solution)/shard_map/sparse_up_both_ways/pallas_call | solution.py:338
  69.7 0.6 copy.10
  70.3 0.6 copy.11
  70.9 0.8 %copy.12 = f32[2,5,128,128]{3,2,1,0:T(8,128)} copy(f32[2,5,128,128]{3,2,1,0:T(8,128)S(1)} %get-tuple-element.14) | data formatting | bytes 1310720
Async XLA Ops:
  0.6 0.8 %copy-start = (bf16[128,256]{1,0:T(8,128)(2,1)S(1)}, bf16[128,256]{1,0:T(8,128)(2,1)}, u32[]{:S(2)}) copy-start(bf16[128,256]{1,0:T(8,128)(2,1)} %cot_hbm.1) | copy-start | bytes 196612
  1.5 0.7 copy-start.1
  2.2 0.7 copy-start.2
